TPU v7x, 32 devices: a whole 2x2x4 slice. The times are simulated.
32 devices in a mesh: dp: 4 (over x, core), inner: 2 (over y), outer: 4 (over z).
Axes of the slice: x: 2, y: 2, z: 4, core: 2. Of those that a mesh axis runs over, the one named last changes fastest.
Arguments:
- partials: bfloat16 [32, 120, 16384], P(('dp', 'inner', 'outer')), parts along dimension 0, may hold values from -5 to 5
- residual: bfloat16 [480, 16384], P('dp', ('inner', 'outer')), parts along dimension 0, may hold values from -18 to 18
- norm_gain: float32 [16384], replicated, may hold values from 0.25 to 1.75
- kv_weight: bfloat16 [16384, 8, 256], P(None, ('inner', 'outer')), may hold values from -0.046875 to 0.046875
Outputs:
- stream: bfloat16 [480, 16384], P('dp', ('inner', 'outer')), parts along dimension 0
- kv_pair: bfloat16 [480, 8, 256], P('dp', ('inner', 'outer')), parts along dimension 0
There are 4 independent parts, one for each index of `dp`. A program takes and returns all parts, laid end to end along the dimension named above; an argument that names none is the same for every part. Nothing has to cross between parts.
All inputs are finite; a program needn't handle non-finite values.
Results may differ from a plain program's by a relative error of at most 0.015.
Values may be sent and summed in bfloat16 or wider, within the bound.
A program may use at most 128 MiB of HBM per device.

v0:
```python
import jax
import jax.numpy as jnp
from jax import lax
from jax.sharding import PartitionSpec as P


def body(partials, residual, norm_gain, kv_weight):
    own_part = partials[0].astype(jnp.float32)
    half_sum = lax.psum_scatter(
        own_part.astype(jnp.bfloat16), "inner", scatter_dimension=1, tiled=True
    )
    level_one = lax.optimization_barrier(half_sum).astype(jnp.float32)
    level_two = lax.psum_scatter(
        level_one.astype(jnp.bfloat16), "outer", scatter_dimension=1, tiled=True
    ).astype(jnp.float32)
    stream = (residual.astype(jnp.float32) + level_two).astype(jnp.bfloat16)
    values = stream.astype(jnp.float32)
    rows = stream.shape[0]
    width = norm_gain.shape[0]
    local = stream.shape[1]
    heads_local = kv_weight.shape[1]
    pair = kv_weight.shape[2]
    gain_local = lax.dynamic_slice_in_dim(
        norm_gain, lax.axis_index(("inner", "outer")) * local, local
    )
    squares = lax.psum(jnp.sum(values * values, axis=1), ("inner", "outer"))
    factor = lax.rsqrt(squares / width + 1e-05)
    normed = (values * factor[:, None] * gain_local[None, :]).astype(jnp.bfloat16)
    flat_weight = kv_weight.reshape(width, heads_local * pair)
    total = jnp.dot(
        lax.all_gather(normed, ("inner", "outer"), axis=1, tiled=True),
        flat_weight,
        preferred_element_type=jnp.float32,
    )
    kv_pair = total.astype(jnp.bfloat16).reshape(rows, heads_local, pair)
    return (stream, kv_pair)


def solution(mesh):
    placed = (
        P(("dp", "inner", "outer"), None, None),
        P("dp", ("inner", "outer")),
        P(),
        P(None, ("inner", "outer"), None),
    )
    return jax.shard_map(
        body,
        mesh=mesh,
        in_specs=placed,
        out_specs=(P("dp", ("inner", "outer")), P("dp", ("inner", "outer"), None)),
        check_vma=False,
    )
```

profile of v0, /device:TPU:0, one launch (start us, length us, event | category | flops | bytes accessed | tf_op | source)
XLA Modules:
  0.0 211.5 jit_solution(2441227540335786770)
XLA Ops:
  7.2 0.0 copy-start.1
  7.2 0.0 reduce-scatter.3.cloned.1.call-start
  7.2 0.7 reduce-scatter.3.cloned.1.call-update
  7.9 0.0 reduce-scatter.5.cloned.1.call-start
  8.0 57.0 %reduce-scatter.3.cloned.1.call-done = bf16[120,8192]{1,0:T(8,128)(2,1)} async-done(((bf16[120,16384]{1,0:T(8,128)(2,1)}), bf16[120,8192]{1,0:T(8,128)(2,1)}) %reduce-scatter.3.cloned.1.call-update) | async-done | bytes 1966096 | tf_op jit(solution)/shard_map/reduce_scatter | solution.py:9
  65.0 0.0 reduce-scatter.5.cloned.1.call-update
  65.0 0.0 all-gather.2.cloned.1.call-start
  65.0 0.7 dynamic_slice.3
  65.7 43.1 %reduce-scatter.5.cloned.1.call-done = bf16[120,2048]{1,0:T(8,128)(2,1)} async-done(((bf16[120,8192]{1,0:T(8,128)(2,1)}), bf16[120,2048]{1,0:T(8,128)(2,1)}) %reduce-scatter.5.cloned.1.call-update) | async-done | bytes 491536 | tf_op jit(solution)/shard_map/reduce_scatter | solution.py:13
  108.9 0.0 copy-done.1
  108.9 1.3 fusion.8
  110.2 0.0 copy-start
  110.2 19.7 %psum.7 = f32[120]{0:T(128)S(1)} all-reduce(f32[120]{0:T(128)S(1)} %get-tuple-element.2), channel_id=1, replica_groups=mesh['dp'=4,'inner'=2,'outer'=4] {'inner','outer'}, use_global_device_ids=true, to_apply=%region_3.0 | all-reduce | flops 120 | bytes 960 | tf_op jit(solution)/shard_map/psum | solution.py:26
  129.9 1.0 fusion.10
  130.9 0.0 all-gather.2.cloned.1.call-update
  130.9 67.5 %all-gather.2.cloned.1.call-done = bf16[120,16384]{1,0:T(8,128)(2,1)} async-done(((bf16[120,2048]{1,0:T(8,128)(2,1)}), bf16[120,16384]{1,0:T(8,128)(2,1)}) %all-gather.2.cloned.1.call-update) | async-done | bytes 3932176 | tf_op jit(solution)/shard_map/all_gather | solution.py:31
  198.4 6.5 %fusion.5 = bf16[120,1,256]{2,0,1:T(8,128)(2,1)} fusion(bf16[120,16384]{1,0:T(8,128)(2,1)} %all-gather.2.cloned.1.call-done, bf16[16384,1,256]{2,0,1:T(8,128)(2,1)} %param.7), kind=kOutput, calls=%fused_computation.5 | convolution fusion | flops 1006663680 | bytes 12382208 | tf_op jit(solution)/shard_map/dot_general | solution.py:30
  204.9 0.0 copy-done
  (1 shorter events, 0.0 us)
Async XLA Ops:
  7.2 101.7 %copy-start.1 = (bf16[120,2048]{1,0:T(8,128)(2,1)S(1)}, bf16[120,2048]{1,0:T(8,128)(2,1)}, u32[]{:S(2)}) copy-start(bf16[120,2048]{1,0:T(8,128)(2,1)} %param.5) | copy-start | bytes 1474564
  7.2 57.8 %reduce-scatter.3.cloned.1.call-start = ((), (), s32[]{:S(2)}) async-start(), calls=%async_computation.2 | async-start | bytes 5898240 | tf_op jit(solution)/shard_map/reduce_scatter | solution.py:9
  7.9 100.9 %reduce-scatter.5.cloned.1.call-start = ((), (), s32[]{:S(2)}) async-start(), calls=%async_computation.3 | async-start | bytes 2457600 | tf_op jit(solution)/shard_map/reduce_scatter | solution.py:13
  65.0 133.4 %all-gather.2.cloned.1.call-start = ((), (), s32[]{:S(2)}) async-start(), calls=%async_computation.4 | async-start | bytes 4423680 | tf_op jit(solution)/shard_map/all_gather | solution.py:31
  110.2 94.8 %copy-start = (bf16[120,2048]{1,0:T(8,128)(2,1)}, bf16[120,2048]{1,0:T(8,128)(2,1)S(1)}, u32[]{:S(2)}) copy-start(bf16[120,2048]{1,0:T(8,128)(2,1)S(1)} %get-tuple-element.3) | copy-start | bytes 1474564
Sparse Core Ops, SparseCore 0:
  10.2 54.6 reduce-scatter.2
  67.4 41.4 reduce-scatter.4
  131.0 67.3 all-gather.1
where the time goes:
time: 212 us; the launch traced here: 211 us
  waiting for transfers between devices  168 us (79%)
  blocking collectives  19.7 us (9%)
  between operations  13.8 us (7%)
  matrix products  6.52 us (3%)
  other arithmetic  2.28 us (1%)
    all_gather x1, waiting for transfers between devices, body(): lax.all_gather(normed, ('inner', 'outer'), axis=1, tiled=True)  67.5 us
    reduce_scatter x1, waiting for transfers between devices, body(): lax.psum_scatter(own_part.astype(jnp.bfloat16), 'inner', scatter_dimensio...  57 us
    reduce_scatter x1, waiting for transfers between devices, body(): lax.psum_scatter(level_one.astype(jnp.bfloat16), 'outer', scatter_dimensi...  43.1 us
    psum x1, blocking collectives, body(): squares = lax.psum(jnp.sum(values * values, axis=1), ('inner', 'outer'))  19.7 us
    dot_general x1, matrix products, body(): jnp.dot(lax.all_gather(normed, ('inner', 'outer'), axis=1, tiled=True), f...  6.52 us
  transfers between devices with their start and end apart: 3, of which 3 were waited for; matrix products, arithmetic and copies ran while one was open for 0% of the time, Pallas kernels for 0%

commit v1 on v0

v1 whole, which is shorter than its diff:
```python
import functools

import jax
import jax.numpy as jnp
from jax import lax
from jax.experimental import pallas as pl
from jax.experimental.pallas import tpu as pltpu
from jax.sharding import PartitionSpec as P

MESH = pl.DeviceIdType.MESH
F32 = jnp.float32
BF16 = jnp.bfloat16
PIECES = 8
AHEAD = 2


def fused(n, pieces, partials, residual, gain, weight, stream_out, kv_out,
          mine, resid, gains, w, ybuf, rbuf, lbuf, ga, gb, tmp, acc, sq,
          loc, y_s, y_r, r_s, r_r, l_s, l_r, a_r, a_rs, a_ls, a_ys,
          b_r, b_rs, b_ls, b_ys):
    i = lax.axis_index("inner")
    o = lax.axis_index("outer")
    other = 1 - i
    rows, local = resid.shape
    width = gains.shape[1]
    half = n * local
    cols = local // pieces
    cut = cols // 2
    to_y = {"inner": other}
    to_r = {"outer": jnp.minimum(o + 1, n - 1)}
    to_l = {"outer": jnp.maximum(o - 1, 0)}
    has_r = o < n - 1
    has_l = o > 0

    loads = [
        pltpu.make_async_copy(
            partials.at[0, :, pl.ds(pl.multiple_of(i * half, half), half)], mine, loc.at[0]
        ),
        pltpu.make_async_copy(residual, resid, loc.at[1]),
        pltpu.make_async_copy(gain, gains, loc.at[2]),
        pltpu.make_async_copy(weight, w, loc.at[3]),
    ]

    def remote(src, dst, ssem, rsem, to):
        return pltpu.make_async_remote_copy(
            src_ref=src, dst_ref=dst, send_sem=ssem, recv_sem=rsem,
            device_id=to, device_id_type=MESH,
        )

    def y_copy(d, p):
        at = pl.multiple_of(other * half + d * local + p * cols, cols)
        return remote(partials.at[0, :, pl.ds(at, cols)], ybuf.at[d, p],
                      y_s.at[d, p], y_r.at[d, p], to_y)

    def r_copy(d, p):
        return remote(rbuf.at[d, p], rbuf.at[d, p], r_s.at[d, p], r_r.at[d, p], to_r)

    def l_copy(d, p):
        return remote(lbuf.at[d, p], lbuf.at[d, p], l_s.at[d, p], l_r.at[d, p], to_l)

    def a_copy(c, p, ssem, to):
        t = i * n + c
        return remote(ga.at[t, p], ga.at[t, p], ssem.at[c, p], a_r.at[t, p], to)

    def b_copy(t, p, ssem, to):
        return remote(gb.at[t, p], gb.at[t, p], ssem, b_r.at[t, p], to)

    def inside(p):
        return (p >= 0) & (p < pieces)

    def level_one(d, p):
        y_copy(d, p).wait_recv()
        at = pl.multiple_of(d * local + p * cols, cols)
        return mine[:, pl.ds(at, cols)].astype(F32) + ybuf[d, p].astype(F32)

    def skew(d):
        return jnp.where(d > o, o, jnp.where(d < o, n - 1 - o, n - 1))

    def send_y(s):
        for d in range(n):
            p = s - skew(d)

            @pl.when(inside(p))
            def _():
                y_copy(d, p).start()

    barrier = pltpu.get_barrier_semaphore()
    pl.semaphore_signal(barrier, inc=1, device_id=to_y, device_id_type=MESH)

    @pl.when(has_r)
    def _():
        pl.semaphore_signal(barrier, inc=1, device_id=to_r, device_id_type=MESH)

    @pl.when(has_l)
    def _():
        pl.semaphore_signal(barrier, inc=1, device_id=to_l, device_id_type=MESH)

    pl.semaphore_wait(barrier, 1 + has_r.astype(jnp.int32) + has_l.astype(jnp.int32))
    for s in range(AHEAD):
        send_y(jnp.int32(s))
    for load in loads:
        load.start()
    acc[...] = jnp.zeros_like(acc)
    sq[...] = jnp.zeros_like(sq)
    for load in loads[:3]:
        load.wait()

    def passing(s):
        p = s - o

        @pl.when(inside(p) & has_r)
        def _():
            for d in reversed(range(n)):
                @pl.when(d > o)
                def _():
                    value = level_one(d, p)

                    @pl.when(has_l)
                    def _():
                        r_copy(d, p).wait_recv()
                        rbuf[d, p] = (value + rbuf[d, p].astype(F32)).astype(BF16)

                    @pl.when(jnp.logical_not(has_l))
                    def _():
                        rbuf[d, p] = value.astype(BF16)

                    r_copy(d, p).start()

        q = s - (n - 1 - o)

        @pl.when(inside(q) & has_l)
        def _():
            for d in range(n):
                @pl.when(d < o)
                def _():
                    value = level_one(d, q)

                    @pl.when(has_r)
                    def _():
                        l_copy(d, q).wait_recv()
                        lbuf[d, q] = (value + lbuf[d, q].astype(F32)).astype(BF16)

                    @pl.when(jnp.logical_not(has_r))
                    def _():
                        lbuf[d, q] = value.astype(BF16)

                    l_copy(d, q).start()

    def finish(s):
        p = s - (n - 1)

        @pl.when(inside(p))
        def _():
            at = pl.multiple_of(p * cols, cols)
            tmp[...] = level_one(o, p) + resid[:, pl.ds(at, cols)].astype(F32)

            @pl.when(has_l)
            def _():
                r_copy(o, p).wait_recv()
                tmp[...] += rbuf[o, p].astype(F32)

            @pl.when(has_r)
            def _():
                l_copy(o, p).wait_recv()
                tmp[...] += lbuf[o, p].astype(F32)

            value = tmp[...].astype(BF16)
            stream_out[:, pl.ds(at, cols)] = value
            me = i * n + o
            ga[me, p] = value[:, :cut]
            gb[me, p] = value[:, cut:]
            b_copy(me, p, b_ys.at[p], to_y).start()

    def spread(s, far):
        for c in range(n):
            p = s - (n - 1) - jnp.abs(o - c) - far
            t = (other if far else i) * n + c

            @pl.when(inside(p))
            def _():
                if far:
                    a_in = remote(ga.at[t, p], ga.at[t, p], a_ys.at[c, p], a_r.at[t, p], to_y)
                    a_in.wait_recv()
                    b_copy(t, p, b_ys.at[p], to_y).wait_recv()
                else:
                    @pl.when(c != o)
                    def _():
                        a_copy(c, p, a_ys, to_y).wait_recv()
                        b_copy(t, p, b_ys.at[p], to_y).wait_recv()
                    a_copy(c, p, a_ys, to_y).start()

                @pl.when((c <= o) & has_r)
                def _():
                    if not far:
                        a_copy(c, p, a_rs, to_r).start()
                    b_copy(t, p, b_rs.at[t, p], to_r).start()

                @pl.when((c >= o) & has_l)
                def _():
                    if not far:
                        a_copy(c, p, a_ls, to_l).start()
                    b_copy(t, p, b_ls.at[t, p], to_l).start()

    def multiply(s):
        @pl.loop(0, 2 * n)
        def _(k):
            far = (k >= n).astype(jnp.int32)
            c = k - far * n
            p = s - (n - 1) - jnp.abs(o - c) - far
            t = jnp.where(far > 0, other, i) * n + c

            @pl.when(inside(p))
            def _():
                at = pl.multiple_of(t * local + p * cols, cols)
                value = jnp.concatenate([ga[t, p], gb[t, p]], axis=1).astype(F32)
                square = value * value
                part = square[:, :128]
                for j in range(1, cols // 128):
                    part += square[:, j * 128:(j + 1) * 128]
                sq[...] += part
                scaled = (value * gains[:, pl.ds(at, cols)]).astype(BF16)
                acc[...] += jnp.dot(
                    scaled, w[pl.ds(at, cols), :], preferred_element_type=F32
                )

    @pl.loop(0, pieces + 2 * n - 1)
    def _(s):
        send_y(s + AHEAD)
        passing(s)
        finish(s)
        spread(s, 0)
        spread(s, 1)

        @pl.when(s == n - 1)
        def _():
            loads[3].wait()

        multiply(s)

    factor = lax.rsqrt(jnp.sum(sq[...], axis=1, keepdims=True) / width + 1e-05)
    kv_out[...] = (acc[...] * factor).astype(BF16)

    @pl.loop(0, pieces)
    def _(p):
        me = i * n + o
        b_copy(me, p, b_ys.at[p], to_y).wait_send()
        for d in range(n):
            y_copy(d, p).wait_send()
            a_copy(d, p, a_ys, to_y).wait_send()

            @pl.when(d > o)
            def _():
                r_copy(d, p).wait_send()

            @pl.when(d < o)
            def _():
                l_copy(d, p).wait_send()

            @pl.when((d <= o) & has_r)
            def _():
                a_copy(d, p, a_rs, to_r).wait_send()
                for t in (d, n + d):
                    b_copy(t, p, b_rs.at[t, p], to_r).wait_send()

            @pl.when((d >= o) & has_l)
            def _():
                a_copy(d, p, a_ls, to_l).wait_send()
                for t in (d, n + d):
                    b_copy(t, p, b_ls.at[t, p], to_l).wait_send()


def body(n, partials, residual, norm_gain, kv_weight):
    rows, local = residual.shape
    width = norm_gain.shape[0]
    heads_local, pair = kv_weight.shape[1:]
    pieces = PIECES
    cols = local // pieces
    wide = heads_local * pair
    dma = pltpu.SemaphoreType.DMA
    vmem = pltpu.VMEM
    stream, kv = pl.pallas_call(
        functools.partial(fused, n, pieces),
        out_shape=(
            jax.ShapeDtypeStruct((rows, local), BF16),
            jax.ShapeDtypeStruct((rows, wide), BF16),
        ),
        in_specs=[pl.BlockSpec(memory_space=pl.ANY)] * 4,
        out_specs=(pl.BlockSpec(memory_space=pltpu.VMEM),) * 2,
        scratch_shapes=[
            vmem((rows, n * local), BF16),
            vmem((rows, local), BF16),
            vmem((1, width), F32),
            vmem((width, wide), BF16),
            vmem((n, pieces, rows, cols), BF16),
            vmem((n, pieces, rows, cols), BF16),
            vmem((n, pieces, rows, cols), BF16),
            vmem((2 * n, pieces, rows, cols // 2), BF16),
            vmem((2 * n, pieces, rows, cols // 2), BF16),
            vmem((rows, cols), F32),
            vmem((rows, wide), F32),
            vmem((rows, 128), F32),
            dma((4,)),
            dma((n, pieces)), dma((n, pieces)),
            dma((n, pieces)), dma((n, pieces)),
            dma((n, pieces)), dma((n, pieces)),
            dma((2 * n, pieces)),
            dma((n, pieces)), dma((n, pieces)), dma((n, pieces)),
            dma((2 * n, pieces)),
            dma((2 * n, pieces)), dma((2 * n, pieces)), dma((pieces,)),
        ],
        compiler_params=pltpu.CompilerParams(
            collective_id=0, has_side_effects=True, vmem_limit_bytes=60 * 1024 * 1024
        ),
        cost_estimate=pl.CostEstimate(
            flops=2 * rows * width * wide,
            bytes_accessed=2 * (rows * width + width * wide),
            transcendentals=rows,
        ),
    )(partials, residual, norm_gain.reshape(1, width), kv_weight.reshape(width, wide))
    return stream, kv.reshape(rows, heads_local, pair)


def solution(mesh):
    placed = (
        P(("dp", "inner", "outer"), None, None),
        P("dp", ("inner", "outer")),
        P(),
        P(None, ("inner", "outer"), None),
    )
    return jax.shard_map(
        functools.partial(body, mesh.shape["outer"]),
        mesh=mesh,
        in_specs=placed,
        out_specs=(P("dp", ("inner", "outer")), P("dp", ("inner", "outer"), None)),
        check_vma=False,
    )
```

time: 212 us -> 99.3 us (0.47)
  waiting for transfers between devices: 168 us -> 0 us
  Pallas kernels: 0 us -> 95.2 us
  blocking collectives: 19.7 us -> 0 us
  between operations: 13.8 us -> 0.64 us
  matrix products: 6.52 us -> 0 us
  local copies, waits for them, and re-layouts: 0.71 us -> 3.31 us
  other arithmetic: 2.28 us -> 0 us
    reduce_scatter x2 -> x0, waiting for transfers between devices: 100 us -> none  [the longest x1 57 us: body(): lax.psum_scatter(own_part.astype(jnp.bfloat16), 'inner', scatter_dimensio...]
    pallas_call x0 -> x1, Pallas kernels: none -> 95.2 us  [body(): pl.pallas_call(functools.partial(fused, n, pieces), out_shape=(jax.ShapeD...]
    all_gather x1 -> x0, waiting for transfers between devices: 67.5 us -> none  [body(): lax.all_gather(normed, ('inner', 'outer'), axis=1, tiled=True)]
    psum x1 -> x0, blocking collectives: 19.7 us -> none  [body(): squares = lax.psum(jnp.sum(values * values, axis=1), ('inner', 'outer'))]
    dot_general x1 -> x0, matrix products: 6.52 us -> none  [body(): jnp.dot(lax.all_gather(normed, ('inner', 'outer'), axis=1, tiled=True), f...]
    unnamed x4 -> x2, local copies, waits for them, and re-layouts: 0.01 us -> 3.31 us
  transfers between devices with their start and end apart: 3 -> 0, of which waited for: 3 -> 0; matrix products, arithmetic and copies ran while one was open for 0% -> 0% of each run, Pallas kernels for 0% -> 0%
where the time goes in v1:
time: 99.3 us; the launch traced here: 99.1 us
  Pallas kernels  95.2 us (96%)
  local copies, waits for them, and re-layouts  3.31 us (3%)
    pallas_call x1, Pallas kernels, body(): pl.pallas_call(functools.partial(fused, n, pieces), out_shape=(jax.ShapeD...  95.2 us
    unnamed x2, local copies, waits for them, and re-layouts  3.31 us

profile of v1, /device:TPU:0, one launch (start us, length us, event | category | flops | bytes accessed | tf_op | source)
XLA Modules:
  0.0 99.1 jit_solution(2725975454979169848)
XLA Ops:
  0.6 95.2 %shard_map.59 = (bf16[120,2048]{1,0:T(8,128)(2,1)}, bf16[120,256]{1,0:T(8,128)(2,1)}) custom-call(bf16[1,120,16384]{2,1,0:T(8,128)(2,1)} %partials.1, bf16[120,2048]{1,0:T(8,128)(2,1)} %residual.1, f32[1,16384]{1,0:T(1,128)} %bitcast.4, bf16[16384,256]{1,0:T(8,128)(2,1)} %bitcast.3), custom_call_target="tpu_custom_call" | custom-call | flops 1006632960 | bytes 12320768 | tf_op jit(solution)/shard_map/pallas_call | solution.py:281
  95.8 1.9 %copy.8 = bf16[120,2048]{1,0:T(8,128)(2,1)} copy(bf16[120,2048]{1,0:T(8,128)(2,1)} %get-tuple-element.8) | data formatting | bytes 983040
  97.6 1.5 %copy.9 = bf16[120,1,256]{2,0,1:T(8,128)(2,1)} copy(bf16[120,1,256]{2,0,1:T(8,128)(2,1)} %bitcast.5) | data formatting | bytes 122880

commit v2 on v1

--- a/solution.py
+++ b/solution.py
@@ -11,7 +11,7 @@
 F32 = jnp.float32
 BF16 = jnp.bfloat16
 PIECES = 8
-AHEAD = 2
+AHEAD = 11
 
 
 def fused(n, pieces, partials, residual, gain, weight, stream_out, kv_out,

time: 99.3 us -> 115 us (1.16)
  Pallas kernels: 95.2 us -> 111 us
    pallas_call x1, Pallas kernels: 95.2 us -> 111 us  [body(): pl.pallas_call(functools.partial(fused, n, pieces), out_shape=(jax.ShapeD...]
where the time goes in v2:
time: 115 us
  Pallas kernels  111 us (97%)
  local copies, waits for them, and re-layouts  3.31 us (3%)
    pallas_call x1, Pallas kernels, body(): pl.pallas_call(functools.partial(fused, n, pieces), out_shape=(jax.ShapeD...  111 us
    unnamed x2, local copies, waits for them, and re-layouts  3.31 us

profile of v2, /device:TPU:0, one launch (start us, length us, event | category | flops | bytes accessed | tf_op | source)
XLA Modules:
  0.0 115.0 jit_solution(7440316678683622046)
XLA Ops:
  0.6 111.1 %shard_map.59 = (bf16[120,2048]{1,0:T(8,128)(2,1)}, bf16[120,256]{1,0:T(8,128)(2,1)}) custom-call(bf16[1,120,16384]{2,1,0:T(8,128)(2,1)} %partials.1, bf16[120,2048]{1,0:T(8,128)(2,1)} %residual.1, f32[1,16384]{1,0:T(1,128)} %bitcast.4, bf16[16384,256]{1,0:T(8,128)(2,1)} %bitcast.3), custom_call_target="tpu_custom_call" | custom-call | flops 1006632960 | bytes 12320768 | tf_op jit(solution)/shard_map/pallas_call | solution.py:281
  111.7 1.9 %copy.8 = bf16[120,2048]{1,0:T(8,128)(2,1)} copy(bf16[120,2048]{1,0:T(8,128)(2,1)} %get-tuple-element.8) | data formatting | bytes 983040
  113.5 1.5 %copy.9 = bf16[120,1,256]{2,0,1:T(8,128)(2,1)} copy(bf16[120,1,256]{2,0,1:T(8,128)(2,1)} %bitcast.5) | data formatting | bytes 122880

commit v3 on v1

--- a/solution.py
+++ b/solution.py
@@ -225,11 +225,11 @@
 
     @pl.loop(0, pieces + 2 * n - 1)
     def _(s):
-        send_y(s + AHEAD)
         passing(s)
         finish(s)
         spread(s, 0)
         spread(s, 1)
+        send_y(s + AHEAD)
 
         @pl.when(s == n - 1)
         def _():

time: 99.3 us -> 99.9 us (level)
  no operation moved by 1% of the time
where the time goes in v3:
time: 99.9 us; the launch traced here: 99.7 us
  Pallas kernels  95.8 us (96%)
  local copies, waits for them, and re-layouts  3.31 us (3%)
    pallas_call x1, Pallas kernels, body(): pl.pallas_call(functools.partial(fused, n, pieces), out_shape=(jax.ShapeD...  95.8 us
    unnamed x2, local copies, waits for them, and re-layouts  3.31 us

profile of v3, /device:TPU:0, one launch (start us, length us, event | category | flops | bytes accessed | tf_op | source)
XLA Modules:
  0.0 99.7 jit_solution(6318254636973705168)
XLA Ops:
  0.6 95.8 %shard_map.59 = (bf16[120,2048]{1,0:T(8,128)(2,1)}, bf16[120,256]{1,0:T(8,128)(2,1)}) custom-call(bf16[1,120,16384]{2,1,0:T(8,128)(2,1)} %partials.1, bf16[120,2048]{1,0:T(8,128)(2,1)} %residual.1, f32[1,16384]{1,0:T(1,128)} %bitcast.4, bf16[16384,256]{1,0:T(8,128)(2,1)} %bitcast.3), custom_call_target="tpu_custom_call" | custom-call | flops 1006632960 | bytes 12320768 | tf_op jit(solution)/shard_map/pallas_call | solution.py:281
  96.4 1.9 %copy.8 = bf16[120,2048]{1,0:T(8,128)(2,1)} copy(bf16[120,2048]{1,0:T(8,128)(2,1)} %get-tuple-element.8) | data formatting | bytes 983040
  98.3 1.5 %copy.9 = bf16[120,1,256]{2,0,1:T(8,128)(2,1)} copy(bf16[120,1,256]{2,0,1:T(8,128)(2,1)} %bitcast.5) | data formatting | bytes 122880

commit v4 on v2

--- a/solution.py
+++ b/solution.py
@@ -10,14 +10,15 @@
 MESH = pl.DeviceIdType.MESH
 F32 = jnp.float32
 BF16 = jnp.bfloat16
-PIECES = 8
-AHEAD = 11
+PIECES = 16
+AHEAD = 3
+CYCLE = 2
+EARLY = 1
 
 
 def fused(n, pieces, partials, residual, gain, weight, stream_out, kv_out,
-          mine, resid, gains, w, ybuf, rbuf, lbuf, ga, gb, tmp, acc, sq,
-          loc, y_s, y_r, r_s, r_r, l_s, l_r, a_r, a_rs, a_ls, a_ys,
-          b_r, b_rs, b_ls, b_ys):
+          mine, resid, gains, w, ybuf, rbuf, lbuf, g, tmp, acc, sq,
+          loc, out_s, y_r, r_r, l_r, g_r):
     i = lax.axis_index("inner")
     o = lax.axis_index("outer")
     other = 1 - i
@@ -25,7 +26,8 @@
     width = gains.shape[1]
     half = n * local
     cols = local // pieces
-    cut = cols // 2
+    group = max(1, 256 // cols)
+    early = sum(p % CYCLE < EARLY for p in range(pieces))
     to_y = {"inner": other}
     to_r = {"outer": jnp.minimum(o + 1, n - 1)}
     to_l = {"outer": jnp.maximum(o - 1, 0)}
@@ -50,23 +52,23 @@
     def y_copy(d, p):
         at = pl.multiple_of(other * half + d * local + p * cols, cols)
         return remote(partials.at[0, :, pl.ds(at, cols)], ybuf.at[d, p],
-                      y_s.at[d, p], y_r.at[d, p], to_y)
+                      out_s.at[0], y_r.at[d, p], to_y)
 
     def r_copy(d, p):
-        return remote(rbuf.at[d, p], rbuf.at[d, p], r_s.at[d, p], r_r.at[d, p], to_r)
+        return remote(rbuf.at[d, p], rbuf.at[d, p], out_s.at[1], r_r.at[d, p], to_r)
 
     def l_copy(d, p):
-        return remote(lbuf.at[d, p], lbuf.at[d, p], l_s.at[d, p], l_r.at[d, p], to_l)
-
-    def a_copy(c, p, ssem, to):
-        t = i * n + c
-        return remote(ga.at[t, p], ga.at[t, p], ssem.at[c, p], a_r.at[t, p], to)
-
-    def b_copy(t, p, ssem, to):
-        return remote(gb.at[t, p], gb.at[t, p], ssem, b_r.at[t, p], to)
+        return remote(lbuf.at[d, p], lbuf.at[d, p], out_s.at[1], l_r.at[d, p], to_l)
+
+    def g_copy(t, p, kind, to):
+        k = t * pieces + p
+        return remote(g.at[k], g.at[k], out_s.at[kind], g_r.at[k], to)
 
     def inside(p):
         return (p >= 0) & (p < pieces)
+
+    def is_early(p):
+        return lax.rem(p, CYCLE) < EARLY
 
     def level_one(d, p):
         y_copy(d, p).wait_recv()
@@ -95,11 +97,12 @@
     def _():
         pl.semaphore_signal(barrier, inc=1, device_id=to_l, device_id_type=MESH)
 
+    for load in loads[:3]:
+        load.start()
     pl.semaphore_wait(barrier, 1 + has_r.astype(jnp.int32) + has_l.astype(jnp.int32))
     for s in range(AHEAD):
         send_y(jnp.int32(s))
-    for load in loads:
-        load.start()
+    loads[3].start()
     acc[...] = jnp.zeros_like(acc)
     sq[...] = jnp.zeros_like(sq)
     for load in loads[:3]:
@@ -167,60 +170,73 @@
             value = tmp[...].astype(BF16)
             stream_out[:, pl.ds(at, cols)] = value
             me = i * n + o
-            ga[me, p] = value[:, :cut]
-            gb[me, p] = value[:, cut:]
-            b_copy(me, p, b_ys.at[p], to_y).start()
-
-    def spread(s, far):
+            g[me * pieces + p] = value
+
+            @pl.when(is_early(p))
+            def _():
+                g_copy(me, p, 2, to_y).start()
+
+    def along(c, t, p, kind):
+        @pl.when((c <= o) & has_r)
+        def _():
+            g_copy(t, p, kind, to_r).start()
+
+        @pl.when((c >= o) & has_l)
+        def _():
+            g_copy(t, p, kind, to_l).start()
+
+    def near(s):
         for c in range(n):
-            p = s - (n - 1) - jnp.abs(o - c) - far
-            t = (other if far else i) * n + c
+            p = s - (n - 1) - jnp.abs(o - c)
+            t = i * n + c
 
             @pl.when(inside(p))
             def _():
-                if far:
-                    a_in = remote(ga.at[t, p], ga.at[t, p], a_ys.at[c, p], a_r.at[t, p], to_y)
-                    a_in.wait_recv()
-                    b_copy(t, p, b_ys.at[p], to_y).wait_recv()
-                else:
-                    @pl.when(c != o)
-                    def _():
-                        a_copy(c, p, a_ys, to_y).wait_recv()
-                        b_copy(t, p, b_ys.at[p], to_y).wait_recv()
-                    a_copy(c, p, a_ys, to_y).start()
-
-                @pl.when((c <= o) & has_r)
-                def _():
-                    if not far:
-                        a_copy(c, p, a_rs, to_r).start()
-                    b_copy(t, p, b_rs.at[t, p], to_r).start()
-
-                @pl.when((c >= o) & has_l)
-                def _():
-                    if not far:
-                        a_copy(c, p, a_ls, to_l).start()
-                    b_copy(t, p, b_ls.at[t, p], to_l).start()
+                @pl.when(c != o)
+                def _():
+                    g_copy(t, p, 3, to_r).wait_recv()
+
+                along(c, t, p, 3)
+
+                @pl.when(jnp.logical_not(is_early(p)))
+                def _():
+                    g_copy(t, p, 2, to_y).start()
+
+    def far(s):
+        for c in range(n):
+            p = s - n - jnp.abs(o - c)
+            t = other * n + c
+
+            @pl.when(inside(p))
+            def _():
+                g_copy(t, p, 2, to_y).wait_recv()
+
+                @pl.when(is_early(p))
+                def _():
+                    along(c, t, p, 4)
 
     def multiply(s):
         @pl.loop(0, 2 * n)
         def _(k):
-            far = (k >= n).astype(jnp.int32)
-            c = k - far * n
-            p = s - (n - 1) - jnp.abs(o - c) - far
-            t = jnp.where(far > 0, other, i) * n + c
-
-            @pl.when(inside(p))
-            def _():
-                at = pl.multiple_of(t * local + p * cols, cols)
-                value = jnp.concatenate([ga[t, p], gb[t, p]], axis=1).astype(F32)
+            away = (k >= n).astype(jnp.int32)
+            c = k - away * n
+            p = s - (n - 1) - jnp.abs(o - c) - away
+            t = jnp.where(away > 0, other, i) * n + c
+
+            @pl.when(inside(p) & (lax.rem(p, group) == group - 1))
+            def _():
+                first = p - (group - 1)
+                at = pl.multiple_of(t * local + first * cols, group * cols)
+                parts = [g[t * pieces + first + j] for j in range(group)]
+                value = jnp.concatenate(parts, axis=1).astype(F32)
                 square = value * value
                 part = square[:, :128]
-                for j in range(1, cols // 128):
+                for j in range(1, group * cols // 128):
                     part += square[:, j * 128:(j + 1) * 128]
                 sq[...] += part
-                scaled = (value * gains[:, pl.ds(at, cols)]).astype(BF16)
+                scaled = (value * gains[:, pl.ds(at, group * cols)]).astype(BF16)
                 acc[...] += jnp.dot(
-                    scaled, w[pl.ds(at, cols), :], preferred_element_type=F32
+                    scaled, w[pl.ds(at, group * cols), :], preferred_element_type=F32
                 )
 
     @pl.loop(0, pieces + 2 * n - 1)
@@ -228,8 +244,8 @@
         send_y(s + AHEAD)
         passing(s)
         finish(s)
-        spread(s, 0)
-        spread(s, 1)
+        near(s)
+        far(s)
 
         @pl.when(s == n - 1)
         def _():
@@ -240,33 +256,22 @@
     factor = lax.rsqrt(jnp.sum(sq[...], axis=1, keepdims=True) / width + 1e-05)
     kv_out[...] = (acc[...] * factor).astype(BF16)
 
-    @pl.loop(0, pieces)
-    def _(p):
-        me = i * n + o
-        b_copy(me, p, b_ys.at[p], to_y).wait_send()
-        for d in range(n):
-            y_copy(d, p).wait_send()
-            a_copy(d, p, a_ys, to_y).wait_send()
-
-            @pl.when(d > o)
-            def _():
-                r_copy(d, p).wait_send()
-
-            @pl.when(d < o)
-            def _():
-                l_copy(d, p).wait_send()
-
-            @pl.when((d <= o) & has_r)
-            def _():
-                a_copy(d, p, a_rs, to_r).wait_send()
-                for t in (d, n + d):
-                    b_copy(t, p, b_rs.at[t, p], to_r).wait_send()
-
-            @pl.when((d >= o) & has_l)
-            def _():
-                a_copy(d, p, a_ls, to_l).wait_send()
-                for t in (d, n + d):
-                    b_copy(t, p, b_ls.at[t, p], to_l).wait_send()
+    def sent(ref, kind):
+        remote(ref, ref, out_s.at[kind], g_r.at[0], to_y).wait_send()
+
+    sent(ybuf, 0)
+    sent(rbuf.at[pl.ds(0, n - 1)], 1)
+    sent(g.at[pl.ds(0, n * (pieces - early) + early)], 2)
+
+    @pl.when(has_l & has_r)
+    def _():
+        sent(g.at[pl.ds(0, (n + 1) * pieces)], 3)
+        sent(g.at[pl.ds(0, (n + 1) * early)], 4)
+
+    @pl.when(jnp.logical_not(has_l & has_r))
+    def _():
+        sent(g.at[pl.ds(0, pieces)], 3)
+        sent(g.at[pl.ds(0, early)], 4)
 
 
 def body(n, partials, residual, norm_gain, kv_weight):
@@ -294,19 +299,16 @@
             vmem((n, pieces, rows, cols), BF16),
             vmem((n, pieces, rows, cols), BF16),
             vmem((n, pieces, rows, cols), BF16),
-            vmem((2 * n, pieces, rows, cols // 2), BF16),
-            vmem((2 * n, pieces, rows, cols // 2), BF16),
+            vmem((2 * n * pieces, rows, cols), BF16),
             vmem((rows, cols), F32),
             vmem((rows, wide), F32),
             vmem((rows, 128), F32),
             dma((4,)),
-            dma((n, pieces)), dma((n, pieces)),
-            dma((n, pieces)), dma((n, pieces)),
-            dma((n, pieces)), dma((n, pieces)),
-            dma((2 * n, pieces)),
-            dma((n, pieces)), dma((n, pieces)), dma((n, pieces)),
-            dma((2 * n, pieces)),
-            dma((2 * n, pieces)), dma((2 * n, pieces)), dma((pieces,)),
+            dma((5,)),
+            dma((n, pieces)),
+            dma((n, pieces)),
+            dma((n, pieces)),
+            dma((2 * n * pieces,)),
         ],
         compiler_params=pltpu.CompilerParams(
             collective_id=0, has_side_effects=True, vmem_limit_bytes=60 * 1024 * 1024

time: 115 us -> 97.6 us (0.85)
  Pallas kernels: 111 us -> 93.5 us
    pallas_call x1, Pallas kernels: 111 us -> 93.5 us  [body(): pl.pallas_call(functools.partial(fused, n, pieces), out_shape=(jax.ShapeD...]
where the time goes in v4:
time: 97.6 us; the launch traced here: 97.4 us
  Pallas kernels  93.5 us (96%)
  local copies, waits for them, and re-layouts  3.31 us (3%)
    pallas_call x1, Pallas kernels, body(): pl.pallas_call(functools.partial(fused, n, pieces), out_shape=(jax.ShapeD...  93.5 us
    unnamed x2, local copies, waits for them, and re-layouts  3.31 us

profile of v4, /device:TPU:0, one launch (start us, length us, event | category | flops | bytes accessed | tf_op | source)
XLA Modules:
  0.0 97.4 jit_solution(14132932439573820010)
XLA Ops:
  0.6 93.5 %shard_map.59 = (bf16[120,2048]{1,0:T(8,128)(2,1)}, bf16[120,256]{1,0:T(8,128)(2,1)}) custom-call(bf16[1,120,16384]{2,1,0:T(8,128)(2,1)} %partials.1, bf16[120,2048]{1,0:T(8,128)(2,1)} %residual.1, f32[1,16384]{1,0:T(1,128)} %bitcast.4, bf16[16384,256]{1,0:T(8,128)(2,1)} %bitcast.3), custom_call_target="tpu_custom_call" | custom-call | flops 1006632960 | bytes 12320768 | tf_op jit(solution)/shard_map/pallas_call | solution.py:286
  94.1 1.9 %copy.8 = bf16[120,2048]{1,0:T(8,128)(2,1)} copy(bf16[120,2048]{1,0:T(8,128)(2,1)} %get-tuple-element.8) | data formatting | bytes 983040
  95.9 1.5 %copy.9 = bf16[120,1,256]{2,0,1:T(8,128)(2,1)} copy(bf16[120,1,256]{2,0,1:T(8,128)(2,1)} %bitcast.5) | data formatting | bytes 122880

commit v5 on v4

--- a/solution.py
+++ b/solution.py
@@ -12,8 +12,8 @@
 BF16 = jnp.bfloat16
 PIECES = 16
 AHEAD = 3
-CYCLE = 2
-EARLY = 1
+CYCLE = 3
+EARLY = 2
 
 
 def fused(n, pieces, partials, residual, gain, weight, stream_out, kv_out,

time: 97.6 us -> 97.8 us (level)
  no operation moved by 1% of the time
where the time goes in v5:
time: 97.8 us; the launch traced here: 97.6 us
  Pallas kernels  93.6 us (96%)
  local copies, waits for them, and re-layouts  3.31 us (3%)
    pallas_call x1, Pallas kernels, body(): pl.pallas_call(functools.partial(fused, n, pieces), out_shape=(jax.ShapeD...  93.6 us
    unnamed x2, local copies, waits for them, and re-layouts  3.31 us

profile of v5, /device:TPU:0, one launch (start us, length us, event | category | flops | bytes accessed | tf_op | source)
XLA Modules:
  0.0 97.6 jit_solution(4481960822981111865)
XLA Ops:
  0.6 93.6 %shard_map.59 = (bf16[120,2048]{1,0:T(8,128)(2,1)}, bf16[120,256]{1,0:T(8,128)(2,1)}) custom-call(bf16[1,120,16384]{2,1,0:T(8,128)(2,1)} %partials.1, bf16[120,2048]{1,0:T(8,128)(2,1)} %residual.1, f32[1,16384]{1,0:T(1,128)} %bitcast.4, bf16[16384,256]{1,0:T(8,128)(2,1)} %bitcast.3), custom_call_target="tpu_custom_call" | custom-call | flops 1006632960 | bytes 12320768 | tf_op jit(solution)/shard_map/pallas_call | solution.py:286
  94.2 1.9 %copy.8 = bf16[120,2048]{1,0:T(8,128)(2,1)} copy(bf16[120,2048]{1,0:T(8,128)(2,1)} %get-tuple-element.8) | data formatting | bytes 983040
  96.1 1.5 %copy.9 = bf16[120,1,256]{2,0,1:T(8,128)(2,1)} copy(bf16[120,1,256]{2,0,1:T(8,128)(2,1)} %bitcast.5) | data formatting | bytes 122880

commit v6 on v0

v6 whole, which is shorter than its diff:
```python
import functools

import jax
import jax.numpy as jnp
from jax import lax
from jax.experimental import pallas as pl
from jax.experimental.pallas import tpu as pltpu
from jax.sharding import PartitionSpec as P

MESH = pl.DeviceIdType.MESH
F32 = jnp.float32
BF16 = jnp.bfloat16
PIECES = 16
AHEAD = 3
CYCLE = 3
EARLY = 1


def fused(n, pieces, partials, residual, gain, weight, stream_out, kv_out,
          mine, resid, gains, w, ybuf, z1_out, z1_in, z2_out, z2_in, g, acc, sq,
          loc, out_s, y_r, hop_r):
    i = lax.axis_index("inner")
    o = lax.axis_index("outer")
    other = 1 - i
    par = lax.rem(o, 2)
    high = o // 2
    rows, local = resid.shape
    width = gains.shape[1]
    half = n * local
    cols = local // pieces
    group = max(1, 256 // cols)
    early = sum(p % CYCLE < EARLY for p in range(pieces))
    to_y = {"inner": other}
    to_1 = {"outer": o + 1 - 2 * par}
    to_2 = {"outer": o + 2 - 4 * high}

    loads = [
        pltpu.make_async_copy(
            partials.at[0, :, pl.ds(pl.multiple_of(i * half, half), half)], mine, loc.at[0]
        ),
        pltpu.make_async_copy(residual, resid, loc.at[1]),
        pltpu.make_async_copy(gain, gains, loc.at[2]),
        pltpu.make_async_copy(weight, w, loc.at[3]),
    ]

    def remote(src, dst, ssem, rsem, to):
        return pltpu.make_async_remote_copy(
            src_ref=src, dst_ref=dst, send_sem=ssem, recv_sem=rsem,
            device_id=to, device_id_type=MESH,
        )

    def y_copy(d, p):
        at = pl.multiple_of(other * half + d * local + p * cols, cols)
        return remote(partials.at[0, :, pl.ds(at, cols)], ybuf.at[d, p],
                      out_s.at[0], y_r.at[d, p], to_y)

    def z1_copy(p):
        return remote(z1_out.at[p], z1_in.at[p], out_s.at[1], hop_r.at[0, p], to_1)

    def z2_copy(p):
        return remote(z2_out.at[p], z2_in.at[p], out_s.at[2], hop_r.at[1, p], to_2)

    def place(side, odd, p):
        return ((side * 2 + odd) * pieces + p) * 2

    def one(side, odd, up, p, kind, hop, to):
        ref = g.at[pl.ds(place(side, odd, p) + up, 1)]
        return remote(ref, ref, out_s.at[kind], hop_r.at[hop, p], to)

    def two(side, odd, p, kind, hop, to):
        ref = g.at[pl.ds(place(side, odd, p), 2)]
        return remote(ref, ref, out_s.at[kind], hop_r.at[hop, p], to)

    def inside(p):
        return (p >= 0) & (p < pieces)

    def is_early(p):
        return lax.rem(p, CYCLE) < EARLY

    def level_one(d, p):
        at = pl.multiple_of(d * local + p * cols, cols)
        return mine[:, pl.ds(at, cols)].astype(F32) + ybuf[d, p].astype(F32)

    def send_y(s):
        @pl.when(inside(s))
        def _():
            for k in range(2):
                y_copy(2 * k + 1 - par, s).start()

        @pl.when(inside(s - 1))
        def _():
            for k in range(2):
                y_copy(2 * k + par, s - 1).start()

    barrier = pltpu.get_barrier_semaphore()
    for to in (to_y, to_1, to_2):
        pl.semaphore_signal(barrier, inc=1, device_id=to, device_id_type=MESH)
    for load in loads[:3]:
        load.start()
    pl.semaphore_wait(barrier, 3)
    for s in range(AHEAD):
        send_y(jnp.int32(s))
    loads[3].start()
    acc[...] = jnp.zeros_like(acc)
    sq[...] = jnp.zeros_like(sq)
    for load in loads[:3]:
        load.wait()

    def stage_0(p):
        for k in range(2):
            d = 2 * k + 1 - par
            y_copy(d, p).wait_recv()
            z1_out[p, k] = level_one(d, p).astype(BF16)
        z1_copy(p).start()

    def stage_1(p):
        for k in range(2):
            y_copy(2 * k + par, p).wait_recv()
        z1_copy(p).wait_recv()
        up = 1 - high
        value = level_one(2 * up + par, p) + z1_in[p, up].astype(F32)
        z2_out[p] = value.astype(BF16)
        z2_copy(p).start()

    def stage_2(p):
        z2_copy(p).wait_recv()
        at = pl.multiple_of(p * cols, cols)
        value = level_one(o, p) + z1_in[p, high].astype(F32) + z2_in[p].astype(F32)
        value = (value + resid[:, pl.ds(at, cols)].astype(F32)).astype(BF16)
        stream_out[:, pl.ds(at, cols)] = value
        g[place(i, par, p) + high] = value
        one(i, par, high, p, 3, 2, to_2).start()

        @pl.when(is_early(p))
        def _():
            one(i, par, high, p, 5, 4, to_y).start()

    def stage_3(p):
        one(i, par, 1 - high, p, 3, 2, to_2).wait_recv()
        two(i, par, p, 4, 3, to_1).start()

        @pl.when(is_early(p))
        def _():
            one(other, par, high, p, 5, 4, to_y).wait_recv()
            one(other, par, high, p, 6, 6, to_2).start()

        @pl.when(jnp.logical_not(is_early(p)))
        def _():
            two(i, par, p, 5, 4, to_y).start()

    def stage_4(p):
        two(i, 1 - par, p, 4, 3, to_1).wait_recv()

        @pl.when(is_early(p))
        def _():
            one(other, par, 1 - high, p, 6, 6, to_2).wait_recv()
            two(other, par, p, 7, 7, to_1).start()

        @pl.when(jnp.logical_not(is_early(p)))
        def _():
            two(i, 1 - par, p, 5, 5, to_y).start()
            two(other, par, p, 5, 4, to_y).wait_recv()

    def stage_5(p):
        @pl.when(is_early(p))
        def _():
            two(other, 1 - par, p, 7, 7, to_1).wait_recv()

        @pl.when(jnp.logical_not(is_early(p)))
        def _():
            two(other, 1 - par, p, 5, 5, to_y).wait_recv()

    def multiply(s):
        @pl.loop(0, 4)
        def _(k):
            away = k // 2
            flip = lax.rem(k, 2)
            side = i + away * (1 - 2 * i)
            odd = par + flip * (1 - 2 * par)
            p = s - 3 - away - flip

            @pl.when(inside(p) & (lax.rem(p, group) == group - 1))
            def _():
                first = p - (group - 1)
                total = acc[...]
                squares = sq[...]
                for up in range(2):
                    t = side * n + 2 * up + odd
                    at = pl.multiple_of(t * local + first * cols, group * cols)
                    parts = [g[place(side, odd, first + j) + up] for j in range(group)]
                    value = jnp.concatenate(parts, axis=1).astype(F32)
                    square = value * value
                    for j in range(group * cols // 128):
                        squares += square[:, j * 128:(j + 1) * 128]
                    scaled = (value * gains[:, pl.ds(at, group * cols)]).astype(BF16)
                    total += jnp.dot(
                        scaled, w[pl.ds(at, group * cols), :], preferred_element_type=F32
                    )
                sq[...] = squares
                acc[...] = total

    @pl.loop(0, pieces + 5)
    def _(s):
        send_y(s + AHEAD)
        for k, stage in enumerate((stage_0, stage_1, stage_2, stage_3, stage_4, stage_5)):
            @pl.when(inside(s - k))
            def _():
                stage(s - k)

        @pl.when(s == 3)
        def _():
            loads[3].wait()

        multiply(s)

    factor = lax.rsqrt(jnp.sum(sq[...], axis=1, keepdims=True) / width + 1e-05)
    kv_out[...] = (acc[...] * factor).astype(BF16)

    def sent(ref, kind):
        remote(ref, ref, out_s.at[kind], hop_r.at[0, 0], to_y).wait_send()

    sent(ybuf, 0)
    sent(z1_out, 1)
    sent(z2_out, 2)
    sent(g.at[pl.ds(0, pieces)], 3)
    sent(g.at[pl.ds(0, 2 * pieces)], 4)
    sent(g.at[pl.ds(0, 4 * (pieces - early) + early)], 5)
    sent(g.at[pl.ds(0, early)], 6)
    sent(g.at[pl.ds(0, 2 * early)], 7)


def body(n, partials, residual, norm_gain, kv_weight):
    rows, local = residual.shape
    width = norm_gain.shape[0]
    heads_local, pair = kv_weight.shape[1:]
    pieces = PIECES
    cols = local // pieces
    wide = heads_local * pair
    dma = pltpu.SemaphoreType.DMA
    vmem = pltpu.VMEM
    stream, kv = pl.pallas_call(
        functools.partial(fused, n, pieces),
        out_shape=(
            jax.ShapeDtypeStruct((rows, local), BF16),
            jax.ShapeDtypeStruct((rows, wide), BF16),
        ),
        in_specs=[pl.BlockSpec(memory_space=pl.ANY)] * 4,
        out_specs=(pl.BlockSpec(memory_space=pltpu.VMEM),) * 2,
        scratch_shapes=[
            vmem((rows, n * local), BF16),
            vmem((rows, local), BF16),
            vmem((1, width), F32),
            vmem((width, wide), BF16),
            vmem((n, pieces, rows, cols), BF16),
            vmem((pieces, 2, rows, cols), BF16),
            vmem((pieces, 2, rows, cols), BF16),
            vmem((pieces, rows, cols), BF16),
            vmem((pieces, rows, cols), BF16),
            vmem((2 * n * pieces, rows, cols), BF16),
            vmem((rows, wide), F32),
            vmem((rows, 128), F32),
            dma((4,)),
            dma((8,)),
            dma((n, pieces)),
            dma((8, pieces)),
        ],
        compiler_params=pltpu.CompilerParams(
            collective_id=0, has_side_effects=True, vmem_limit_bytes=60 * 1024 * 1024
        ),
        cost_estimate=pl.CostEstimate(
            flops=2 * rows * width * wide,
            bytes_accessed=2 * (rows * width + width * wide),
            transcendentals=rows,
        ),
    )(partials, residual, norm_gain.reshape(1, width), kv_weight.reshape(width, wide))
    return stream, kv.reshape(rows, heads_local, pair)


def solution(mesh):
    placed = (
        P(("dp", "inner", "outer"), None, None),
        P("dp", ("inner", "outer")),
        P(),
        P(None, ("inner", "outer"), None),
    )
    return jax.shard_map(
        functools.partial(body, mesh.shape["outer"]),
        mesh=mesh,
        in_specs=placed,
        out_specs=(P("dp", ("inner", "outer")), P("dp", ("inner", "outer"), None)),
        check_vma=False,
    )
```

time: 212 us -> 101 us (0.48)
  waiting for transfers between devices: 168 us -> 0 us
  Pallas kernels: 0 us -> 96.6 us
  blocking collectives: 19.7 us -> 0 us
  between operations: 13.8 us -> 0.64 us
  matrix products: 6.52 us -> 0 us
  local copies, waits for them, and re-layouts: 0.71 us -> 3.31 us
  other arithmetic: 2.28 us -> 0 us
    reduce_scatter x2 -> x0, waiting for transfers between devices: 100 us -> none  [the longest x1 57 us: body(): lax.psum_scatter(own_part.astype(jnp.bfloat16), 'inner', scatter_dimensio...]
    pallas_call x0 -> x1, Pallas kernels: none -> 96.6 us  [body(): pl.pallas_call(functools.partial(fused, n, pieces), out_shape=(jax.ShapeD...]
    all_gather x1 -> x0, waiting for transfers between devices: 67.5 us -> none  [body(): lax.all_gather(normed, ('inner', 'outer'), axis=1, tiled=True)]
    psum x1 -> x0, blocking collectives: 19.7 us -> none  [body(): squares = lax.psum(jnp.sum(values * values, axis=1), ('inner', 'outer'))]
    dot_general x1 -> x0, matrix products: 6.52 us -> none  [body(): jnp.dot(lax.all_gather(normed, ('inner', 'outer'), axis=1, tiled=True), f...]
    unnamed x4 -> x2, local copies, waits for them, and re-layouts: 0.01 us -> 3.31 us
  transfers between devices with their start and end apart: 3 -> 0, of which waited for: 3 -> 0; matrix products, arithmetic and copies ran while one was open for 0% -> 0% of each run, Pallas kernels for 0% -> 0%
where the time goes in v6:
time: 101 us
  Pallas kernels  96.6 us (96%)
  local copies, waits for them, and re-layouts  3.31 us (3%)
    pallas_call x1, Pallas kernels, body(): pl.pallas_call(functools.partial(fused, n, pieces), out_shape=(jax.ShapeD...  96.6 us
    unnamed x2, local copies, waits for them, and re-layouts  3.31 us

profile of v6, /device:TPU:0, one launch (start us, length us, event | category | flops | bytes accessed | tf_op | source)
XLA Modules:
  0.0 100.6 jit_solution(11696383774496029523)
XLA Ops:
  0.6 96.6 %shard_map.59 = (bf16[120,2048]{1,0:T(8,128)(2,1)}, bf16[120,256]{1,0:T(8,128)(2,1)}) custom-call(bf16[1,120,16384]{2,1,0:T(8,128)(2,1)} %partials.1, bf16[120,2048]{1,0:T(8,128)(2,1)} %residual.1, f32[1,16384]{1,0:T(1,128)} %bitcast.4, bf16[16384,256]{1,0:T(8,128)(2,1)} %bitcast.3), custom_call_target="tpu_custom_call" | custom-call | flops 1006632960 | bytes 12320768 | tf_op jit(solution)/shard_map/pallas_call | solution.py:241
  97.2 1.9 %copy.8 = bf16[120,2048]{1,0:T(8,128)(2,1)} copy(bf16[120,2048]{1,0:T(8,128)(2,1)} %get-tuple-element.8) | data formatting | bytes 983040
  99.1 1.5 %copy.9 = bf16[120,1,256]{2,0,1:T(8,128)(2,1)} copy(bf16[120,1,256]{2,0,1:T(8,128)(2,1)} %bitcast.5) | data formatting | bytes 122880

commit v7 on v6

--- a/solution.py
+++ b/solution.py
@@ -11,7 +11,8 @@
 F32 = jnp.float32
 BF16 = jnp.bfloat16
 PIECES = 16
-AHEAD = 3
+AHEAD = 4
+SLACK = 2
 CYCLE = 3
 EARLY = 1
 
@@ -87,10 +88,10 @@
             for k in range(2):
                 y_copy(2 * k + 1 - par, s).start()
 
-        @pl.when(inside(s - 1))
+        @pl.when(inside(s - SLACK))
         def _():
             for k in range(2):
-                y_copy(2 * k + par, s - 1).start()
+                y_copy(2 * k + par, s - SLACK).start()
 
     barrier = pltpu.get_barrier_semaphore()
     for to in (to_y, to_1, to_2):
@@ -177,7 +178,7 @@
             flip = lax.rem(k, 2)
             side = i + away * (1 - 2 * i)
             odd = par + flip * (1 - 2 * par)
-            p = s - 3 - away - flip
+            p = s - SLACK * (3 + away + flip)
 
             @pl.when(inside(p) & (lax.rem(p, group) == group - 1))
             def _():
@@ -199,15 +200,15 @@
                 sq[...] = squares
                 acc[...] = total
 
-    @pl.loop(0, pieces + 5)
+    @pl.loop(0, pieces + 5 * SLACK)
     def _(s):
         send_y(s + AHEAD)
         for k, stage in enumerate((stage_0, stage_1, stage_2, stage_3, stage_4, stage_5)):
-            @pl.when(inside(s - k))
+            @pl.when(inside(s - SLACK * k))
             def _():
-                stage(s - k)
-
-        @pl.when(s == 3)
+                stage(s - SLACK * k)
+
+        @pl.when(s == 3 * SLACK)
         def _():
             loads[3].wait()
 

time: 101 us -> 98.8 us (0.978)
  Pallas kernels: 96.6 us -> 94.6 us
    pallas_call x1, Pallas kernels: 96.6 us -> 94.6 us  [body(): pl.pallas_call(functools.partial(fused, n, pieces), out_shape=(jax.ShapeD...]
where the time goes in v7:
time: 98.8 us; the launch traced here: 98.6 us
  Pallas kernels  94.6 us (96%)
  local copies, waits for them, and re-layouts  3.31 us (3%)
    pallas_call x1, Pallas kernels, body(): pl.pallas_call(functools.partial(fused, n, pieces), out_shape=(jax.ShapeD...  94.6 us
    unnamed x2, local copies, waits for them, and re-layouts  3.31 us

profile of v7, /device:TPU:0, one launch (start us, length us, event | category | flops | bytes accessed | tf_op | source)
XLA Modules:
  0.0 98.6 jit_solution(10392481898399416311)
XLA Ops:
  0.6 94.6 %shard_map.59 = (bf16[120,2048]{1,0:T(8,128)(2,1)}, bf16[120,256]{1,0:T(8,128)(2,1)}) custom-call(bf16[1,120,16384]{2,1,0:T(8,128)(2,1)} %partials.1, bf16[120,2048]{1,0:T(8,128)(2,1)} %residual.1, f32[1,16384]{1,0:T(1,128)} %bitcast.4, bf16[16384,256]{1,0:T(8,128)(2,1)} %bitcast.3), custom_call_target="tpu_custom_call" | custom-call | flops 1006632960 | bytes 12320768 | tf_op jit(solution)/shard_map/pallas_call | solution.py:242
  95.2 1.9 %copy.8 = bf16[120,2048]{1,0:T(8,128)(2,1)} copy(bf16[120,2048]{1,0:T(8,128)(2,1)} %get-tuple-element.8) | data formatting | bytes 983040
  97.1 1.5 %copy.9 = bf16[120,1,256]{2,0,1:T(8,128)(2,1)} copy(bf16[120,1,256]{2,0,1:T(8,128)(2,1)} %bitcast.5) | data formatting | bytes 122880

commit v8 on v5

--- a/solution.py
+++ b/solution.py
@@ -12,12 +12,12 @@
 BF16 = jnp.bfloat16
 PIECES = 16
 AHEAD = 3
-CYCLE = 3
+CYCLE = 5
 EARLY = 2
 
 
 def fused(n, pieces, partials, residual, gain, weight, stream_out, kv_out,
-          mine, resid, gains, w, ybuf, rbuf, lbuf, g, tmp, acc, sq,
+          mine, resid, gains, w, ybuf, zbuf, rbuf, lbuf, g, tmp, acc, sq,
           loc, out_s, y_r, r_r, l_r, g_r):
     i = lax.axis_index("inner")
     o = lax.axis_index("outer")
@@ -27,7 +27,7 @@
     half = n * local
     cols = local // pieces
     group = max(1, 256 // cols)
-    early = sum(p % CYCLE < EARLY for p in range(pieces))
+    early = sum((2 * p + 2) % CYCLE < EARLY for p in range(pieces))
     to_y = {"inner": other}
     to_r = {"outer": jnp.minimum(o + 1, n - 1)}
     to_l = {"outer": jnp.maximum(o - 1, 0)}
@@ -35,9 +35,7 @@
     has_l = o > 0
 
     loads = [
-        pltpu.make_async_copy(
-            partials.at[0, :, pl.ds(pl.multiple_of(i * half, half), half)], mine, loc.at[0]
-        ),
+        pltpu.make_async_copy(partials.at[0], mine, loc.at[0]),
         pltpu.make_async_copy(residual, resid, loc.at[1]),
         pltpu.make_async_copy(gain, gains, loc.at[2]),
         pltpu.make_async_copy(weight, w, loc.at[3]),
@@ -54,11 +52,16 @@
         return remote(partials.at[0, :, pl.ds(at, cols)], ybuf.at[d, p],
                       out_s.at[0], y_r.at[d, p], to_y)
 
-    def r_copy(d, p):
-        return remote(rbuf.at[d, p], rbuf.at[d, p], out_s.at[1], r_r.at[d, p], to_r)
-
-    def l_copy(d, p):
-        return remote(lbuf.at[d, p], lbuf.at[d, p], out_s.at[1], l_r.at[d, p], to_l)
+    def sum_copy(p):
+        return remote(zbuf.at[p], ybuf.at[o, p], out_s.at[0], y_r.at[o, p], to_y)
+
+    def r_copy(side, d, p):
+        ref = rbuf.at[side, d, p]
+        return remote(ref, ref, out_s.at[1], r_r.at[side, d, p], to_r)
+
+    def l_copy(side, d, p):
+        ref = lbuf.at[side, d, p]
+        return remote(ref, ref, out_s.at[1], l_r.at[side, d, p], to_l)
 
     def g_copy(t, p, kind, to):
         k = t * pieces + p
@@ -68,12 +71,15 @@
         return (p >= 0) & (p < pieces)
 
     def is_early(p):
-        return lax.rem(p, CYCLE) < EARLY
+        return lax.rem(2 * p + 2, CYCLE) < EARLY
+
+    def part(side, d, p):
+        at = pl.multiple_of(side * half + d * local + p * cols, cols)
+        return mine[:, pl.ds(at, cols)].astype(F32)
 
     def level_one(d, p):
         y_copy(d, p).wait_recv()
-        at = pl.multiple_of(d * local + p * cols, cols)
-        return mine[:, pl.ds(at, cols)].astype(F32) + ybuf[d, p].astype(F32)
+        return part(i, d, p) + ybuf[d, p].astype(F32)
 
     def skew(d):
         return jnp.where(d > o, o, jnp.where(d < o, n - 1 - o, n - 1))
@@ -82,7 +88,7 @@
         for d in range(n):
             p = s - skew(d)
 
-            @pl.when(inside(p))
+            @pl.when(inside(p) & jnp.logical_not(is_early(p)))
             def _():
                 y_copy(d, p).start()
 
@@ -100,7 +106,7 @@
     for load in loads[:3]:
         load.start()
     pl.semaphore_wait(barrier, 1 + has_r.astype(jnp.int32) + has_l.astype(jnp.int32))
-    for s in range(AHEAD):
+    for s in range(AHEAD - 1):
         send_y(jnp.int32(s))
     loads[3].start()
     acc[...] = jnp.zeros_like(acc)
@@ -108,65 +114,77 @@
     for load in loads[:3]:
         load.wait()
 
+    def hand_on(value, buf, copy, has_before, side, d, p):
+        @pl.when(has_before)
+        def _():
+            copy(side, d, p).wait_recv()
+            buf[side, d, p] = (value + buf[side, d, p].astype(F32)).astype(BF16)
+
+        @pl.when(jnp.logical_not(has_before))
+        def _():
+            buf[side, d, p] = value.astype(BF16)
+
+        copy(side, d, p).start()
+
     def passing(s):
-        p = s - o
-
-        @pl.when(inside(p) & has_r)
-        def _():
-            for d in reversed(range(n)):
-                @pl.when(d > o)
-                def _():
-                    value = level_one(d, p)
-
-                    @pl.when(has_l)
+        for lead in range(2):
+            p = s - o + lead
+            mode = is_early(p) if lead else jnp.logical_not(is_early(p))
+
+            @pl.when(inside(p) & has_r & mode)
+            def _():
+                for d in reversed(range(n)):
+                    @pl.when(d > o)
                     def _():
-                        r_copy(d, p).wait_recv()
-                        rbuf[d, p] = (value + rbuf[d, p].astype(F32)).astype(BF16)
-
-                    @pl.when(jnp.logical_not(has_l))
+                        if lead:
+                            for side in range(2):
+                                hand_on(part(side, d, p), rbuf, r_copy, has_l, side, d, p)
+                        else:
+                            hand_on(level_one(d, p), rbuf, r_copy, has_l, i, d, p)
+
+        for lead in range(2):
+            q = s - (n - 1 - o) + lead
+            mode = is_early(q) if lead else jnp.logical_not(is_early(q))
+
+            @pl.when(inside(q) & has_l & mode)
+            def _():
+                for d in range(n):
+                    @pl.when(d < o)
                     def _():
-                        rbuf[d, p] = value.astype(BF16)
-
-                    r_copy(d, p).start()
-
-        q = s - (n - 1 - o)
-
-        @pl.when(inside(q) & has_l)
-        def _():
-            for d in range(n):
-                @pl.when(d < o)
-                def _():
-                    value = level_one(d, q)
-
-                    @pl.when(has_r)
-                    def _():
-                        l_copy(d, q).wait_recv()
-                        lbuf[d, q] = (value + lbuf[d, q].astype(F32)).astype(BF16)
-
-                    @pl.when(jnp.logical_not(has_r))
-                    def _():
-                        lbuf[d, q] = value.astype(BF16)
-
-                    l_copy(d, q).start()
+                        if lead:
+                            for side in range(2):
+                                hand_on(part(side, d, q), lbuf, l_copy, has_r, side, d, q)
+                        else:
+                            hand_on(level_one(d, q), lbuf, l_copy, has_r, i, d, q)
+
+    def add_passed(side, p):
+        @pl.when(has_l)
+        def _():
+            r_copy(side, o, p).wait_recv()
+            tmp[...] += rbuf[side, o, p].astype(F32)
+
+        @pl.when(has_r)
+        def _():
+            l_copy(side, o, p).wait_recv()
+            tmp[...] += lbuf[side, o, p].astype(F32)
 
     def finish(s):
+        early_p = s - (n - 1) + 1
+
+        @pl.when(inside(early_p) & is_early(early_p))
+        def _():
+            tmp[...] = part(other, o, early_p)
+            add_passed(other, early_p)
+            zbuf[early_p] = tmp[...].astype(BF16)
+            sum_copy(early_p).start()
+
         p = s - (n - 1)
 
         @pl.when(inside(p))
         def _():
             at = pl.multiple_of(p * cols, cols)
             tmp[...] = level_one(o, p) + resid[:, pl.ds(at, cols)].astype(F32)
-
-            @pl.when(has_l)
-            def _():
-                r_copy(o, p).wait_recv()
-                tmp[...] += rbuf[o, p].astype(F32)
-
-            @pl.when(has_r)
-            def _():
-                l_copy(o, p).wait_recv()
-                tmp[...] += lbuf[o, p].astype(F32)
-
+            add_passed(i, p)
             value = tmp[...].astype(BF16)
             stream_out[:, pl.ds(at, cols)] = value
             me = i * n + o
@@ -239,8 +257,9 @@
                     scaled, w[pl.ds(at, group * cols), :], preferred_element_type=F32
                 )
 
-    @pl.loop(0, pieces + 2 * n - 1)
-    def _(s):
+    @pl.loop(0, pieces + 2 * n)
+    def _(step):
+        s = step - 1
         send_y(s + AHEAD)
         passing(s)
         finish(s)
@@ -259,8 +278,8 @@
     def sent(ref, kind):
         remote(ref, ref, out_s.at[kind], g_r.at[0], to_y).wait_send()
 
-    sent(ybuf, 0)
-    sent(rbuf.at[pl.ds(0, n - 1)], 1)
+    sent(g.at[pl.ds(0, n * (pieces - early) + early)], 0)
+    sent(g.at[pl.ds(0, (n - 1) * (pieces + early))], 1)
     sent(g.at[pl.ds(0, n * (pieces - early) + early)], 2)
 
     @pl.when(has_l & has_r)
@@ -292,13 +311,14 @@
         in_specs=[pl.BlockSpec(memory_space=pl.ANY)] * 4,
         out_specs=(pl.BlockSpec(memory_space=pltpu.VMEM),) * 2,
         scratch_shapes=[
-            vmem((rows, n * local), BF16),
+            vmem((rows, width), BF16),
             vmem((rows, local), BF16),
             vmem((1, width), F32),
             vmem((width, wide), BF16),
             vmem((n, pieces, rows, cols), BF16),
-            vmem((n, pieces, rows, cols), BF16),
-            vmem((n, pieces, rows, cols), BF16),
+            vmem((pieces, rows, cols), BF16),
+            vmem((2, n, pieces, rows, cols), BF16),
+            vmem((2, n, pieces, rows, cols), BF16),
             vmem((2 * n * pieces, rows, cols), BF16),
             vmem((rows, cols), F32),
             vmem((rows, wide), F32),
@@ -306,8 +326,8 @@
             dma((4,)),
             dma((5,)),
             dma((n, pieces)),
-            dma((n, pieces)),
-            dma((n, pieces)),
+            dma((2, n, pieces)),
+            dma((2, n, pieces)),
             dma((2 * n * pieces,)),
         ],
         compiler_params=pltpu.CompilerParams(

time: 97.8 us -> 102 us (1.043)
  Pallas kernels: 93.6 us -> 98 us
    pallas_call x1, Pallas kernels: 93.6 us -> 98 us  [body(): pl.pallas_call(functools.partial(fused, n, pieces), out_shape=(jax.ShapeD...]
where the time goes in v8:
time: 102 us
  Pallas kernels  98 us (96%)
  local copies, waits for them, and re-layouts  3.31 us (3%)
    pallas_call x1, Pallas kernels, body(): pl.pallas_call(functools.partial(fused, n, pieces), out_shape=(jax.ShapeD...  98 us
    unnamed x2, local copies, waits for them, and re-layouts  3.31 us

profile of v8, /device:TPU:0, one launch (start us, length us, event | category | flops | bytes accessed | tf_op | source)
XLA Modules:
  0.0 101.9 jit_solution(18136713784145682631)
XLA Ops:
  0.6 98.0 %shard_map.59 = (bf16[120,2048]{1,0:T(8,128)(2,1)}, bf16[120,256]{1,0:T(8,128)(2,1)}) custom-call(bf16[1,120,16384]{2,1,0:T(8,128)(2,1)} %partials.1, bf16[120,2048]{1,0:T(8,128)(2,1)} %residual.1, f32[1,16384]{1,0:T(1,128)} %bitcast.4, bf16[16384,256]{1,0:T(8,128)(2,1)} %bitcast.3), custom_call_target="tpu_custom_call" | custom-call | flops 1006632960 | bytes 12320768 | tf_op jit(solution)/shard_map/pallas_call | solution.py:305
  98.6 1.9 %copy.8 = bf16[120,2048]{1,0:T(8,128)(2,1)} copy(bf16[120,2048]{1,0:T(8,128)(2,1)} %get-tuple-element.8) | data formatting | bytes 983040
  100.5 1.5 %copy.9 = bf16[120,1,256]{2,0,1:T(8,128)(2,1)} copy(bf16[120,1,256]{2,0,1:T(8,128)(2,1)} %bitcast.5) | data formatting | bytes 122880

commit v9 on v4

--- a/solution.py
+++ b/solution.py
@@ -10,8 +10,8 @@
 MESH = pl.DeviceIdType.MESH
 F32 = jnp.float32
 BF16 = jnp.bfloat16
-PIECES = 16
-AHEAD = 3
+PIECES = 8
+AHEAD = 2
 CYCLE = 2
 EARLY = 1
 
@@ -272,6 +272,17 @@
     def _():
         sent(g.at[pl.ds(0, pieces)], 3)
         sent(g.at[pl.ds(0, early)], 4)
+
+
+def write_out(stream, kv, stream_out, kv_out, sems):
+    copies = [
+        pltpu.make_async_copy(stream, stream_out, sems.at[0]),
+        pltpu.make_async_copy(kv, kv_out, sems.at[1]),
+    ]
+    for copy in copies:
+        copy.start()
+    for copy in copies:
+        copy.wait()
 
 
 def body(n, partials, residual, norm_gain, kv_weight):
@@ -319,6 +330,16 @@
             transcendentals=rows,
         ),
     )(partials, residual, norm_gain.reshape(1, width), kv_weight.reshape(width, wide))
+    stream, kv = pl.pallas_call(
+        write_out,
+        out_shape=(
+            jax.ShapeDtypeStruct((rows, local), BF16),
+            jax.ShapeDtypeStruct((rows, wide), BF16),
+        ),
+        in_specs=[pl.BlockSpec(memory_space=pl.ANY)] * 2,
+        out_specs=(pl.BlockSpec(memory_space=pl.ANY),) * 2,
+        scratch_shapes=[dma((2,))],
+    )(stream, kv)
     return stream, kv.reshape(rows, heads_local, pair)
 
 

time: 97.6 us -> 108 us (1.11)
  Pallas kernels: 93.5 us -> 107 us
  local copies, waits for them, and re-layouts: 3.31 us -> 0 us
    pallas_call x0 -> x1, Pallas kernels: none -> 17.9 us  [body(): pl.pallas_call(write_out, out_shape=(jax.ShapeDtypeStruct((rows, local),...]
    pallas_call x1, Pallas kernels: 93.5 us -> 89.4 us  [body(): pl.pallas_call(functools.partial(fused, n, pieces), out_shape=(jax.ShapeD...]
    unnamed x2 -> x0, local copies, waits for them, and re-layouts: 3.31 us -> none
where the time goes in v9:
time: 108 us
  Pallas kernels  107 us (99%)
    pallas_call x1, Pallas kernels, body(): pl.pallas_call(functools.partial(fused, n, pieces), out_shape=(jax.ShapeD...  89.4 us
    pallas_call x1, Pallas kernels, body(): pl.pallas_call(write_out, out_shape=(jax.ShapeDtypeStruct((rows, local),...  17.9 us

profile of v9, /device:TPU:0, one launch (start us, length us, event | category | flops | bytes accessed | tf_op | source)
XLA Modules:
  0.0 107.9 jit_solution(13660927622426603979)
XLA Ops:
  0.6 89.4 %shard_map.59 = (bf16[120,2048]{1,0:T(8,128)(2,1)}, bf16[120,256]{1,0:T(8,128)(2,1)}) custom-call(bf16[1,120,16384]{2,1,0:T(8,128)(2,1)} %partials.1, bf16[120,2048]{1,0:T(8,128)(2,1)} %residual.1, f32[1,16384]{1,0:T(1,128)} %bitcast.4, bf16[16384,256]{1,0:T(8,128)(2,1)} %bitcast.3), custom_call_target="tpu_custom_call" | custom-call | flops 1006632960 | bytes 12320768 | tf_op jit(solution)/shard_map/pallas_call | solution.py:297
  90.0 17.9 %shard_map.60 = (bf16[120,2048]{1,0:T(8,128)(2,1)}, bf16[120,256]{1,0:T(8,128)(2,1)}) custom-call(bf16[120,2048]{1,0:T(8,128)(2,1)} %get-tuple-element.6.stream, bf16[120,256]{1,0:T(8,128)(2,1)} %get-tuple-element.7.kv), custom_call_target="tpu_custom_call" | custom-call | tf_op jit(solution)/shard_map/pallas_call | solution.py:333

commit v10 on v4

--- a/solution.py
+++ b/solution.py
@@ -10,8 +10,8 @@
 MESH = pl.DeviceIdType.MESH
 F32 = jnp.float32
 BF16 = jnp.bfloat16
-PIECES = 16
-AHEAD = 3
+PIECES = 8
+AHEAD = 2
 CYCLE = 2
 EARLY = 1
 

time: 97.6 us -> 93.5 us (0.958)
  Pallas kernels: 93.5 us -> 89.4 us
    pallas_call x1, Pallas kernels: 93.5 us -> 89.4 us  [body(): pl.pallas_call(functools.partial(fused, n, pieces), out_shape=(jax.ShapeD...]
where the time goes in v10:
time: 93.5 us; the launch traced here: 93.3 us
  Pallas kernels  89.4 us (96%)
  local copies, waits for them, and re-layouts  3.31 us (4%)
    pallas_call x1, Pallas kernels, body(): pl.pallas_call(functools.partial(fused, n, pieces), out_shape=(jax.ShapeD...  89.4 us
    unnamed x2, local copies, waits for them, and re-layouts  3.31 us

profile of v10, /device:TPU:0, one launch (start us, length us, event | category | flops | bytes accessed | tf_op | source)
XLA Modules:
  0.0 93.3 jit_solution(5900271013599673766)
XLA Ops:
  0.6 89.4 %shard_map.59 = (bf16[120,2048]{1,0:T(8,128)(2,1)}, bf16[120,256]{1,0:T(8,128)(2,1)}) custom-call(bf16[1,120,16384]{2,1,0:T(8,128)(2,1)} %partials.1, bf16[120,2048]{1,0:T(8,128)(2,1)} %residual.1, f32[1,16384]{1,0:T(1,128)} %bitcast.4, bf16[16384,256]{1,0:T(8,128)(2,1)} %bitcast.3), custom_call_target="tpu_custom_call" | custom-call | flops 1006632960 | bytes 12320768 | tf_op jit(solution)/shard_map/pallas_call | solution.py:286
  90.0 1.9 %copy.8 = bf16[120,2048]{1,0:T(8,128)(2,1)} copy(bf16[120,2048]{1,0:T(8,128)(2,1)} %get-tuple-element.8) | data formatting | bytes 983040
  91.9 1.5 %copy.9 = bf16[120,1,256]{2,0,1:T(8,128)(2,1)} copy(bf16[120,1,256]{2,0,1:T(8,128)(2,1)} %bitcast.5) | data formatting | bytes 122880
